TPU v7x, 256 devices: a whole 4x4x8 slice. The times are simulated.
256 devices in a mesh: col: 128 (over z, x, y), row: 2 (over core).
Axes of the slice: x: 4, y: 4, z: 8, core: 2. Of those that a mesh axis runs over, the one named last changes fastest.
Arguments:
- band_tiles: bfloat16 [2048, 5, 256, 256], P(('col', 'row')), may hold values from -0.125 to 0.125
- band_mask: int32 [2048, 5], P(('col', 'row')), may hold values from 0 to 1, as said below
- panels: bfloat16 [2, 2048, 256, 256], P(None, ('col', 'row')), may hold values from -6 to 6
- panel_seed: bfloat16 [2, 2048, 256, 256], P(None, ('col', 'row')), may hold values from -6 to 6
- diag_inverse: float32 [2, 256, 256], replicated, may hold values from -1.5 to 1.5, as said below
- cross_block: bfloat16 [256, 256], replicated, may hold values from -0.375 to 0.375
- cross_seed: float32 [256, 256], replicated, may hold values from -6 to 6
- diag_seed: float32 [256, 256], replicated, may hold values from -6 to 6
Outputs:
- panel_adjoint: bfloat16 [2, 2048, 256, 256], P(None, ('col', 'row'))
- cross_adjoint: float32 [256, 256], replicated
- diag_adjoint: float32 [256, 256], replicated
Inputs may be any that keep to these rules, and one draw needn't show every extreme that they name: band_mask[c, 0] is 1 for every column c, and band_mask[c, d] is 0 where c + d >= 2048. Each diag_inverse[p] is lower triangular, with diagonal entries between 0.5 and 1.5.
All inputs are finite; a program needn't handle non-finite values.
Results may differ from a plain program's by a relative error of at most 0.0038.
Values may be sent and summed in bfloat16 or wider, within the bound.
A program may use at most 192 MiB of HBM per device.

v0:
```python
import math

import jax
import jax.numpy as jnp
from jax import lax
from jax.sharding import PartitionSpec as P


def padded(cells, sides, width):
    for axis, dim in sides:
        count = lax.axis_size(axis)
        ends = count - 1
        head = lax.slice_in_dim(cells, 0, width, axis=dim)
        tail = lax.slice_in_dim(cells, cells.shape[dim] - width, cells.shape[dim], axis=dim)
        cells = jnp.concatenate(
            [
                lax.ppermute(tail, axis, [(i, (i + 1) % count) for i in range(ends)]),
                cells,
                lax.ppermute(head, axis, [((i + 1) % count, i) for i in range(ends)]),
            ],
            axis=dim,
        )
    return cells


def passed_along(shard, axis, by):
    count = lax.axis_size(axis)
    pairs = [(i, i + by) for i in range(count) if 0 <= i + by < count]
    return lax.ppermute(shard, axis, pairs)


def band_terms(masked, col_rows, below_rows):
    columns = masked.shape[0]
    slot_count = masked.shape[1]
    panel_count = col_rows.shape[0]
    tail_shape = col_rows.shape[2:]
    upper_zero = jnp.zeros((panel_count, columns) + tail_shape, jnp.float32)
    lower_zero = jnp.zeros((panel_count, columns + slot_count - 1) + tail_shape, jnp.float32)
    upper_term = upper_zero
    lower_term = lower_zero
    for offset in range(slot_count):
        slot_tiles = masked[:, offset]
        upper_term = upper_term + jnp.einsum(
            "eab,peak->pebk",
            slot_tiles,
            below_rows[:, offset : offset + columns],
            preferred_element_type=jnp.float32,
        )
        if offset > 0:
            lower_term = lower_term.at[:, offset : offset + columns].add(
                jnp.einsum(
                    "eab,pebk->peak", slot_tiles, col_rows, preferred_element_type=jnp.float32
                )
            )
    return (upper_term, lower_term)


def body(
    band_tiles, band_mask, panels, panel_seed, diag_inverse, cross_block, cross_seed, diag_seed
):
    highest = lax.Precision.HIGHEST
    row_count = panels.shape[1]
    tile_size = panels.shape[2]
    band_width = band_tiles.shape[1] - 1
    trailing = row_count * lax.axis_size("col") * lax.axis_size("row")
    scale_factor = 1.0 / math.sqrt(trailing * tile_size)
    masked = band_tiles * band_mask[:, :, None, None].astype(jnp.bfloat16)
    padded_rows = padded(panels, ((("col", "row"), 1),), band_width)
    rim_tiles = passed_along(masked[row_count - band_width :], ("col", "row"), 1)
    all_tiles = jnp.concatenate([rim_tiles, masked], axis=0)
    upper_term, lower_term = band_terms(
        all_tiles, padded_rows[:, : row_count + band_width], padded_rows
    )
    band_term = upper_term[:, band_width:] + lower_term[:, band_width : band_width + row_count]
    adjoint_one = jnp.einsum(
        "rbk,kl->rbl",
        panel_seed[1].astype(jnp.float32) - band_term[1],
        diag_inverse[1],
        precision=highest,
    )
    zero_rows = panels[0].astype(jnp.float32)
    cross_part = jnp.einsum("rbk,rbl->kl", adjoint_one, zero_rows, precision=highest) * scale_factor
    cross_total = lax.psum(cross_part, ("col", "row"))
    cross_wide = cross_block.astype(jnp.float32)
    carried_cross = jnp.einsum("rbk,kl->rbl", adjoint_one, cross_wide, precision=highest)
    adjoint_zero = jnp.einsum(
        "rbk,kl->rbl",
        panel_seed[0].astype(jnp.float32) - band_term[0] - carried_cross,
        diag_inverse[0],
        precision=highest,
    )
    diag_part = jnp.einsum("rbk,rbl->kl", adjoint_zero, zero_rows, precision=highest) * scale_factor
    diag_total = lax.psum(diag_part, ("col", "row"))
    cross_adjoint = jnp.dot(cross_seed - cross_total, diag_inverse[0], precision=highest)
    diag_adjoint = diag_seed - jnp.dot(cross_adjoint.T, cross_wide, precision=highest) - diag_total
    panel_adjoint = jnp.stack([adjoint_zero, adjoint_one]).astype(jnp.bfloat16)
    return (panel_adjoint, cross_adjoint, diag_adjoint)


def solution(mesh):
    return jax.shard_map(
        body,
        mesh=mesh,
        in_specs=(
            P(("col", "row"), None, None, None),
            P(("col", "row"), None),
            P(None, ("col", "row"), None, None),
            P(None, ("col", "row"), None, None),
            P(),
            P(),
            P(),
            P(),
        ),
        out_specs=(P(None, ("col", "row"), None, None), P(), P()),
        check_vma=False,
    )
```

profile of v0, /device:TPU:1, one launch (start us, length us, event | category | flops | bytes accessed | tf_op | source)
XLA Modules:
  0.0 399.3 jit_solution(1611622413711531655)
XLA Ops:
  8.0 2.9 copy_multiply_fusion
  11.0 2.3 copy-done.1
  15.0 4.6 %collective-permute-start.1 = (bf16[4,5,256,256]{3,2,0,1:T(8,128)(2,1)}, bf16[4,5,256,256]{3,2,0,1:T(8,128)(2,1)}, u32[]{:S(2)}, u32[]{:S(2)}) collective-permute-start(bf16[4,5,256,256]{3,2,0,1:T(8,128)(2,1)} %slice.204), channel_id=1, source_target_pairs={{0,1},{1,2},{2,3},{3,4},{4,5},{5,6},{6,7},{7,8},{8,9},{9,10},{10,1... | collective-permute-start | bytes 7864328 | tf_op jit(solution)/shard_map/ppermute | solution.py:29
  19.5 2.9 copy.12
  25.9 3.8 collective-permute-start.2
  32.1 2.4 copy.31
  34.4 25.2 %collective-permute-done = bf16[2,4,256,256]{2,3,0,1:T(8,128)(2,1)} collective-permute-done((bf16[2,4,256,256]{2,3,0,1:T(8,128)(2,1)}, bf16[2,4,256,256]{2,3,0,1:T(8,128)(2,1)}, u32[]{:S(2)}, u32[]{:S(2)}) %collective-permute-start) | collective-permute-done | bytes 1048608 | tf_op jit(solution)/shard_map/ppermute | solution.py:17
  59.7 2.7 convolution_bitcast_fusion.1
  63.3 2.8 fusion.1
  66.1 3.0 fusion
  69.1 3.2 slice.216
  72.3 5.1 %fusion.48 = f32[12,2,256,256]{3,2,1,0:T(8,128)} fusion(bf16[2,4,256,256]{2,3,0,1:T(8,128)(2,1)} %collective-permute-done.2, bf16[2,8,256,256]{2,3,0,1:T(8,128)(2,1)S(1)} %copy.12, bf16[2,4,256,256]{2,3,0,1:T(8,128)(2,1)} %collective-permute-done, bf16[8,5,256,256]{3,2,0,1:T(8,128)(2,1)S(1)} %bitcast.90, bf16[4,5,256,256]{3,2,0,1:T(8,128)(2,1)} %collective-permute-done.1), kind=kOutput, calls=%fused_computation.69 | convolution fusion | flops 821035008 | bytes 18350080 | tf_op jit(solution)/shard_map/eab,peak->pebk/dot_general | solution.py:43
  77.4 5.0 %fusion.49 = f32[12,2,256,256]{3,2,1,0:T(8,128)} fusion(bf16[2,4,256,256]{2,3,0,1:T(8,128)(2,1)} %collective-permute-done.2, bf16[2,8,256,256]{2,3,0,1:T(8,128)(2,1)S(1)} %copy.12, bf16[2,4,256,256]{2,3,0,1:T(8,128)(2,1)} %collective-permute-done, bf16[8,5,256,256]{3,2,0,1:T(8,128)(2,1)S(1)} %bitcast.90, bf16[4,5,256,256]{3,2,0,1:T(8,128)(2,1)} %collective-permute-done.1), kind=kOutput, calls=%fused_computation.70 | convolution fusion | flops 821035008 | bytes 18350080 | tf_op jit(solution)/shard_map/eab,peak->pebk/dot_general | solution.py:43
  82.3 4.9 %fusion.50 = f32[12,2,256,256]{3,2,1,0:T(8,128)} fusion(bf16[2,4,256,256]{2,3,0,1:T(8,128)(2,1)} %collective-permute-done.2, bf16[2,8,256,256]{2,3,0,1:T(8,128)(2,1)S(1)} %copy.12, bf16[2,4,256,256]{2,3,0,1:T(8,128)(2,1)} %collective-permute-done, bf16[8,5,256,256]{3,2,0,1:T(8,128)(2,1)S(1)} %bitcast.90, bf16[4,5,256,256]{3,2,0,1:T(8,128)(2,1)} %collective-permute-done.1), kind=kOutput, calls=%fused_computation.71 | convolution fusion | flops 821035008 | bytes 18350080 | tf_op jit(solution)/shard_map/eab,peak->pebk/dot_general | solution.py:43
  87.2 5.1 %fusion.22 = f32[12,2,256,256]{3,2,1,0:T(8,128)} fusion(bf16[8,5,256,256]{3,2,0,1:T(8,128)(2,1)S(1)} %bitcast.90, bf16[4,5,256,256]{3,2,0,1:T(8,128)(2,1)} %collective-permute-done.1, bf16[2,8,256,256]{2,3,0,1:T(8,128)(2,1)S(1)} %copy.12, bf16[2,4,256,256]{2,3,0,1:T(8,128)(2,1)} %collective-permute-done), kind=kOutput, calls=%fused_computation.38 | convolution fusion | flops 807665664 | bytes 17301504 | tf_op jit(solution)/shard_map/eab,peak->pebk/dot_general | solution.py:43
  94.6 5.0 %convolution_bitcast_fusion = f32[2,12,256,256]{2,3,0,1:T(8,128)} fusion(bf16[12,256,256,1]{2,1,3,0:T(8,128)(2,1)S(1)} %fusion.28, bf16[2,8,256,256]{2,3,0,1:T(8,128)(2,1)S(1)} %copy.12, bf16[2,4,256,256]{2,3,0,1:T(8,128)(2,1)} %collective-permute-done), kind=kOutput, calls=%fused_computation.22 | convolution fusion | flops 806879232 | bytes 11010048 | tf_op jit(solution)/shard_map/eab,pebk->peak/dot_general | solution.py:51
  99.7 12.1 %add_bitcast_fusion = f32[2,12,256,256]{2,3,0,1:T(8,128)} fusion(f32[12,2,256,256]{3,2,1,0:T(8,128)} %fusion.48, f32[12,2,256,256]{3,2,1,0:T(8,128)} %fusion.49, f32[12,2,256,256]{3,2,1,0:T(8,128)S(1)} %copy-done.2, f32[12,2,256,256]{3,2,1,0:T(8,128)} %fusion.50, bf16[12,256,256,1]{2,1,3,0:T(8,128)(2,1)} %copy-done.3, ...), kind=kOutput, calls=%fused_computation.12 | convolution fusion | flops 813170688 | bytes 36175872 | tf_op jit(solution)/shard_map/eab,peak->pebk/dot_general | solution.py:43
  111.8 5.6 %fusion.2 = f32[2,8,256,256]{2,3,0,1:T(8,128)S(1)} fusion(f32[2,12,256,256]{2,3,0,1:T(8,128)} %convolution_bitcast_fusion, f32[2,12,256,256]{2,3,0,1:T(8,128)} %slice.216, f32[2,12,256,256]{2,3,0,1:T(8,128)} %add_bitcast_fusion), kind=kLoop, calls=%fused_computation.15 | loop fusion | flops 2097152 | bytes 16777216 | tf_op jit(solution)/shard_map/add | solution.py:74
  117.4 3.5 fusion.10
  120.9 2.8 fusion.31
  125.0 4.8 %fusion.14 = f32[8,256,256]{2,1,0:T(8,128)} fusion(f32[8,256,256]{1,2,0:T(8,128)S(1)} %fusion.44, f32[2,8,256,256]{2,3,0,1:T(8,128)S(1)} %fusion.2, bf16[1,8,256,256]{2,3,0,1:T(8,128)(2,1)S(1)} %copy-done.6, f32[2,256,256]{2,1,0:T(8,128)S(1)} %copy-done.8), kind=kOutput, calls=%fused_computation.30 | convolution fusion | flops 1612185600 | bytes 7602176 | tf_op jit(solution)/shard_map/rbk,kl->rbl/dot_general | solution.py:86
  129.8 4.1 %fusion.30 = f32[256,256]{1,0:T(8,128)} fusion(f32[8,256,256]{2,1,0:T(8,128)} %fusion.14, bf16[2,8,256,256]{3,2,1,0:T(8,128)(2,1)S(1)} %copy-done.4), kind=kOutput, calls=%fused_computation.48 | convolution fusion | flops 1610678272 | bytes 3407872 | tf_op jit(solution)/shard_map/rbk,rbl->kl/dot_general | solution.py:92
  137.3 251.7 %all-reduce.4.cloned.1.call-done = (f32[256,256]{1,0:T(8,128)}, f32[256,256]{1,0:T(8,128)}) async-done(((f32[256,256]{1,0:T(8,128)}, f32[256,256]{1,0:T(8,128)}), (f32[256,256]{1,0:T(8,128)}, f32[256,256]{1,0:T(8,128)})) %all-reduce.4.cloned.1.call-update) | async-done | bytes 524304 | tf_op jit(solution)/shard_map/psum | solution.py:83
  390.4 2.1 fusion.29
  (45 shorter events, 17.5 us)
Async XLA Ops:
  7.2 116.5 %copy-start = (bf16[256,256]{1,0:T(8,128)(2,1)S(1)}, bf16[256,256]{1,0:T(8,128)(2,1)}, u32[]{:S(2)}) copy-start(bf16[256,256]{1,0:T(8,128)(2,1)} %param.21) | copy-start | bytes 393220
  7.2 381.8 %all-reduce.4.cloned.1.call-start = ((), (), s32[]{:S(2)}) async-start(), calls=%async_computation | async-start | bytes 1048576 | tf_op jit(solution)/shard_map/psum | solution.py:83
  10.9 2.4 copy-start.1
  15.0 44.7 %collective-permute-start.1 = (bf16[4,5,256,256]{3,2,0,1:T(8,128)(2,1)}, bf16[4,5,256,256]{3,2,0,1:T(8,128)(2,1)}, u32[]{:S(2)}, u32[]{:S(2)}) collective-permute-start(bf16[4,5,256,256]{3,2,0,1:T(8,128)(2,1)} %slice.204), channel_id=1, source_target_pairs={{0,1},{1,2},{2,3},{3,4},{4,5},{5,6},{6,7},{7,8},{8,9},{9,10},{10,1... | collective-permute-start | bytes 7864328 | tf_op jit(solution)/shard_map/ppermute | solution.py:29
  22.4 7.2 %copy-start.7 = (bf16[2,8,256,256]{3,2,1,0:T(8,128)(2,1)S(1)}, bf16[2,8,256,256]{3,2,1,0:T(8,128)(2,1)}, u32[]{:S(2)}) copy-start(bf16[2,8,256,256]{3,2,1,0:T(8,128)(2,1)} %param.19) | copy-start | bytes 6291460
  24.0 35.7 %collective-permute-start = (bf16[2,4,256,256]{2,3,0,1:T(8,128)(2,1)}, bf16[2,4,256,256]{2,3,0,1:T(8,128)(2,1)}, u32[]{:S(2)}, u32[]{:S(2)}) collective-permute-start(bf16[2,4,256,256]{2,3,0,1:T(8,128)(2,1)} %get-tuple-element.56), channel_id=1, source_target_pairs={{0,1},{1,2},{2,3},{3,4},{4,5},{5,6},{6,7},{7,8},{8,9},{9,10},{10,1... | collective-permute-start | bytes 3145736 | tf_op jit(solution)/shard_map/ppermute | solution.py:17
  25.9 46.4 %collective-permute-start.2 = (bf16[2,4,256,256]{2,3,0,1:T(8,128)(2,1)}, bf16[2,4,256,256]{2,3,0,1:T(8,128)(2,1)}, u32[]{:S(2)}, u32[]{:S(2)}) collective-permute-start(bf16[2,4,256,256]{2,3,0,1:T(8,128)(2,1)} %get-tuple-element.55), channel_id=1, source_target_pairs={{1,0},{2,1},{3,2},{4,3},{5,4},{6,5},{7,6},{8,7},{9,8},{10,9},{11,1... | collective-permute-start | bytes 3145736 | tf_op jit(solution)/shard_map/ppermute | solution.py:19
  32.1 31.2 %slice-start = ((s8[5242880]{0:T(1024)(128)(4,1)}), s8[1048576]{0:T(1024)(128)(4,1)S(1)}, s32[]{:S(2)}) async-start(s8[5242880]{0:T(1024)(128)(4,1)} %bitcast.89), calls=%async_computation.1 | async-start | bytes 2097152
  34.4 28.8 %slice-start.1 = ((s8[5242880]{0:T(1024)(128)(4,1)}), s8[4194304]{0:T(1024)(128)(4,1)S(1)}, s32[]{:S(2)}) async-start(s8[5242880]{0:T(1024)(128)(4,1)} %bitcast.89), calls=%async_computation.2 | async-start | bytes 8388608
  93.5 1.1 copy-start.3
  94.6 5.0 %copy-start.2 = (f32[12,2,256,256]{3,2,1,0:T(8,128)S(1)}, f32[12,2,256,256]{3,2,1,0:T(8,128)}, u32[]{:S(2)}) copy-start(f32[12,2,256,256]{3,2,1,0:T(8,128)} %fusion.22) | copy-start | bytes 18874372
  111.8 5.6 %copy-start.5 = (bf16[1,8,256,256]{2,3,0,1:T(8,128)(2,1)S(1)}, bf16[1,8,256,256]{2,3,0,1:T(8,128)(2,1)}, u32[]{:S(2)}) copy-start(bf16[1,8,256,256]{2,3,0,1:T(8,128)(2,1)} %copy.32) | copy-start | bytes 3145732
  111.8 5.6 %copy-start.8 = (f32[2,256,256]{2,1,0:T(8,128)S(1)}, f32[2,256,256]{2,1,0:T(8,128)}, u32[]{:S(2)}) copy-start(f32[2,256,256]{2,1,0:T(8,128)} %param.20) | copy-start | bytes 1572868
  117.4 3.5 copy-start.4
  120.9 4.0 %copy-start.6 = (bf16[1,8,256,256]{2,3,0,1:T(8,128)(2,1)S(1)}, bf16[1,8,256,256]{2,3,0,1:T(8,128)(2,1)}, u32[]{:S(2)}) copy-start(bf16[1,8,256,256]{2,3,0,1:T(8,128)(2,1)} %copy.31) | copy-start | bytes 3145732
  135.8 253.2 %copy-start.10 = (f32[256,256]{1,0:T(8,128)S(1)}, f32[256,256]{1,0:T(8,128)}, u32[]{:S(2)}) copy-start(f32[256,256]{1,0:T(8,128)} %param.22) | copy-start | bytes 786436
  135.8 254.6 %copy-start.11 = (f32[256,256]{1,0:T(8,128)S(1)}, f32[256,256]{1,0:T(8,128)}, u32[]{:S(2)}) copy-start(f32[256,256]{1,0:T(8,128)} %param.23) | copy-start | bytes 786436
  390.3 2.2 copy-start.9
Sparse Core Ops, SparseCore 0:
  134.1 254.8 all-reduce.3
where the time goes:
time: 401 us; the launch traced here: 399 us
  waiting for transfers between devices  277 us (69%)
  matrix products  65.6 us (16%)
  local copies, waits for them, and re-layouts  18.6 us (5%)
  between operations  14.3 us (4%)
  other arithmetic  13.7 us (3%)
  starting transfers between devices  10.3 us (3%)
    psum x1, waiting for transfers between devices, body(): cross_total = lax.psum(cross_part, ('col', 'row'))  252 us
    dot_general x5, matrix products, band_terms(): jnp.einsum('eab,peak->pebk', slot_tiles, below_rows[:, offset:offset + co...  32.2 us
    ppermute x1, waiting for transfers between devices, padded(): lax.ppermute(tail, axis, [(i, (i + 1) % count) for i in range(ends)])  25.2 us
    dot_general x4, matrix products, band_terms(): jnp.einsum('eab,pebk->peak', slot_tiles, col_rows, preferred_element_type...  13.5 us
    unnamed x31, local copies, waits for them, and re-layouts  10.1 us
  transfers between devices with their start and end apart: 4, of which 2 were waited for; matrix products, arithmetic and copies ran while one was open for 6% of the time, Pallas kernels for 0%

commit v1 on v0

v1 whole, which is shorter than its diff:
```python
import functools
import math

import jax
import jax.numpy as jnp
from jax import lax
from jax.experimental import pallas as pl
from jax.experimental.pallas import tpu as pltpu
from jax.sharding import PartitionSpec as P

MESH = pl.DeviceIdType.MESH
F32 = jnp.float32
BF16 = jnp.bfloat16
TILE = 256
WIDE = 512
ROWS = 8
BAND = 4
PLANE_COLS = 16


def dot(a, b):
    return jnp.dot(a, b, preferred_element_type=F32)


def dot_t(a, b):
    return lax.dot_general(a, b, (((0,), (0,)), ((), ())), preferred_element_type=F32)


def exact_dot(a, b):
    return jnp.dot(a, b, precision=lax.Precision.HIGHEST, preferred_element_type=F32)


def split(a):
    high = a.astype(BF16)
    return high, (a - high.astype(F32)).astype(BF16)


def kernel(
    n_col,
    plane_cols,
    scale,
    band_hbm,
    mask,
    panels_hbm,
    seed_hbm,
    diag_inverse,
    cross_block,
    cross_seed,
    diag_seed,
    out_hbm,
    cross_out,
    diag_out,
    tiles,
    rows,
    seeds,
    acc,
    resid,
    left_in,
    total,
    staged,
    got_a,
    got_b,
    got_c,
    mine,
    w_high,
    w_low,
    out_v,
    in_sem,
    halo_send,
    halo_recv,
    part_send,
    part_recv,
    ar_send,
    ar_recv,
    out_sem,
):
    col, row = lax.axis_index("col"), lax.axis_index("row")
    n_dev = 2 * n_col
    index = col * 2 + row
    left, right = lax.rem(index + n_dev - 1, n_dev), lax.rem(index + 1, n_dev)
    left_id = (left // 2, lax.rem(left, 2))
    right_id = (right // 2, lax.rem(right, 2))
    n_a = 2 * plane_cols
    n_b = n_col // plane_cols
    depth, place = col // plane_cols, lax.rem(col, plane_cols)
    me_a = place * 2 + row

    def plane_id(step):
        peer = lax.rem(me_a + step, n_a)
        return peer, (depth * plane_cols + peer // 2, lax.rem(peer, 2))

    def line_id(step):
        return (lax.rem(depth + step, n_b) * plane_cols + place, row)

    def load(source, target, slot):
        copy = pltpu.make_async_copy(source, target, in_sem.at[slot])
        copy.start()
        return copy

    upper, lower = pl.ds(4, 4), pl.ds(0, 4)
    first, second = pl.ds(0, TILE), pl.ds(TILE, TILE)
    loads_hi = [
        load(panels_hbm.at[0, upper], rows.at[upper, :, first], 0),
        load(panels_hbm.at[1, upper], rows.at[upper, :, second], 1),
        load(band_hbm.at[upper], tiles.at[upper], 2),
    ]
    loads_lo = [
        load(panels_hbm.at[0, lower], rows.at[lower, :, first], 3),
        load(panels_hbm.at[1, lower], rows.at[lower, :, second], 4),
        load(band_hbm.at[lower], tiles.at[lower], 5),
        load(seed_hbm.at[0], seeds.at[:, :, first], 6),
        load(seed_hbm.at[1], seeds.at[:, :, second], 7),
    ]

    barrier = pltpu.get_barrier_semaphore()
    pl.semaphore_signal(barrier, inc=1, device_id=left_id, device_id_type=MESH)
    pl.semaphore_signal(barrier, inc=1, device_id=right_id, device_id_type=MESH)

    @pl.loop(1, n_a)
    def _(step):
        pl.semaphore_signal(barrier, inc=1, device_id=plane_id(step)[1], device_id_type=MESH)

    @pl.loop(1, n_b)
    def _(step):
        pl.semaphore_signal(barrier, inc=1, device_id=line_id(step), device_id_type=MESH)

    pl.semaphore_wait(barrier, n_a + n_b)

    halos = []
    for p, lanes in ((0, first), (1, second)):
        halos.append(
            pltpu.make_async_remote_copy(
                src_ref=panels_hbm.at[p, lower],
                dst_ref=rows.at[pl.ds(8, 4), :, lanes],
                send_sem=halo_send.at[p],
                recv_sem=halo_recv.at[p],
                device_id=left_id,
                device_id_type=MESH,
            )
        )
        halos[-1].start()

    def tile(c, d):
        keep = jnp.full((TILE, TILE), mask[c, d].astype(F32), F32).astype(BF16)
        return tiles[c, d] * keep

    def lower_terms(r, slots):
        lhs = jnp.concatenate([tile(r - d, d) for d in slots], axis=1)
        rhs = rows[pl.ds(r - slots[0], len(slots))].reshape(len(slots) * TILE, WIDE)
        return dot(lhs, rhs)

    def upper_terms(i, slots):
        lhs = jnp.concatenate([tile(i, d) for d in slots], axis=0)
        rhs = rows[pl.ds(i + slots[0], len(slots))].reshape(len(slots) * TILE, WIDE)
        return dot_t(lhs, rhs)

    for copy in loads_hi:
        copy.wait()
    parts = []
    for r in (11, 10, 9, 8):
        slots = list(range(4, r - 8, -1))
        resid[r] = (-lower_terms(r, slots)).astype(BF16)
        parts.append(
            pltpu.make_async_remote_copy(
                src_ref=resid.at[r],
                dst_ref=left_in.at[r - 8],
                send_sem=part_send.at[r - 8],
                recv_sem=part_recv.at[r - 8],
                device_id=right_id,
                device_id_type=MESH,
            )
        )
        parts[-1].start()

    inverse_zero, inverse_one = diag_inverse[0], diag_inverse[1]
    cross_wide = cross_block[...].astype(F32)
    through = exact_dot(inverse_one, cross_wide)
    carry = -exact_dot(through, inverse_zero)
    zeros = jnp.zeros((TILE, TILE), F32)
    weights = jnp.concatenate(
        [
            jnp.concatenate([inverse_zero, zeros], axis=1),
            jnp.concatenate([carry, inverse_one], axis=1),
        ],
        axis=0,
    )
    w_high[...], w_low[...] = split(weights)
    cross_base = exact_dot(cross_seed[...], inverse_zero)
    cross_out[...] = cross_base
    diag_out[...] = diag_seed[...] - exact_dot(cross_base.T, cross_wide)

    for copy in loads_lo:
        copy.wait()

    @pl.loop(4, 8)
    def _(i):
        acc[i] = seeds[i].astype(F32) - lower_terms(i, [4, 3, 2, 1])

    total[...] = jnp.zeros_like(total)

    for i in range(4):
        value = seeds[i].astype(F32)
        if i:
            value = value - lower_terms(i, list(range(i, 0, -1)))
        acc[i] = value

    @pl.loop(0, 4)
    def _(i):
        value = acc[i] - upper_terms(i, [0, 1, 2, 3, 4])
        acc[i] = value
        total[...] += dot_t(rows[i, :, :TILE], value.astype(BF16))

    for i in range(4, 8):
        acc[i] = acc[i] - upper_terms(i, list(range(0, 8 - i)))

    for copy in halos:
        copy.wait_recv()
    for i in range(4, 8):
        value = acc[i] - upper_terms(i, list(range(8 - i, 5)))
        resid[i] = value.astype(BF16)

    @pl.loop(4, 12)
    def _(i):
        total[...] += dot_t(rows[i, :, :TILE], resid[i])

    part_rows = WIDE // n_a
    for p in range(2):
        half = total[:, p * TILE : (p + 1) * TILE].astype(BF16)
        staged[pl.ds(p * n_a // 2, n_a // 2)] = half.reshape(n_a // 2, part_rows, TILE)

    @pl.loop(1, n_a)
    def _(step):
        peer, peer_id = plane_id(step)
        pltpu.make_async_remote_copy(
            src_ref=staged.at[peer],
            dst_ref=got_a.at[me_a],
            send_sem=ar_send.at[0],
            recv_sem=ar_recv.at[0],
            device_id=peer_id,
            device_id_type=MESH,
        ).start()

    got_a[me_a] = staged[me_a]

    def solve_rows(begin, end):
        @pl.loop(begin, end)
        def _(i):
            value = resid[i]
            one = value[:, TILE:]
            low, high = w_low, w_high
            zero_term = dot(value, high[:, :TILE]) + dot(value, low[:, :TILE])
            one_term = dot(one, high[TILE:, TILE:]) + dot(one, low[TILE:, TILE:])
            out_v[0, i] = zero_term.astype(BF16)
            out_v[1, i] = one_term.astype(BF16)

        copies = [
            pltpu.make_async_copy(
                out_v.at[p, pl.ds(begin, end - begin)],
                out_hbm.at[p, pl.ds(begin, end - begin)],
                out_sem.at[p, begin // 4],
            )
            for p in range(2)
        ]
        for copy in copies:
            copy.start()
        return copies

    outs = solve_rows(4, 8)

    def wait_bytes(buffer, count, send, recv):
        view = buffer.at[pl.ds(0, count)]
        pltpu.make_async_copy(view, view, recv).wait()
        pltpu.make_async_copy(view, view, send).wait()

    wait_bytes(got_a, n_a - 1, ar_send.at[0], ar_recv.at[0])
    mine[...] = jnp.sum(got_a[...].astype(F32), axis=0).astype(BF16)

    @pl.loop(1, n_b)
    def _(step):
        pltpu.make_async_remote_copy(
            src_ref=mine,
            dst_ref=got_b.at[depth],
            send_sem=ar_send.at[1],
            recv_sem=ar_recv.at[1],
            device_id=line_id(step),
            device_id_type=MESH,
        ).start()

    got_b[depth] = mine[...]

    for copy in parts:
        copy.wait_recv()

    @pl.loop(0, 4)
    def _(i):
        resid[i] = (acc[i] + left_in[i].astype(F32)).astype(BF16)

    wait_bytes(got_b, n_b - 1, ar_send.at[1], ar_recv.at[1])
    got_c[me_a] = jnp.sum(got_b[...].astype(F32), axis=0).astype(BF16)

    @pl.loop(1, n_a)
    def _(step):
        pltpu.make_async_remote_copy(
            src_ref=got_c.at[me_a],
            dst_ref=got_c.at[me_a],
            send_sem=ar_send.at[2],
            recv_sem=ar_recv.at[2],
            device_id=plane_id(step)[1],
            device_id_type=MESH,
        ).start()

    outs += solve_rows(0, 4)

    wait_bytes(got_c, n_a - 1, ar_send.at[2], ar_recv.at[2])
    zero_sum = got_c[pl.ds(0, n_a // 2)].reshape(TILE, TILE)
    one_sum = got_c[pl.ds(n_a // 2, n_a // 2)].reshape(TILE, TILE).astype(F32)
    inverse_zero, inverse_one = diag_inverse[0], diag_inverse[1]
    turned = exact_dot(one_sum, inverse_one).T
    cross_out[...] -= scale * exact_dot(turned, inverse_zero)
    mixed = exact_dot(one_sum, exact_dot(inverse_one, cross_block[...].astype(F32)))
    inner = mixed + mixed.T - zero_sum.astype(F32).T
    diag_out[...] += scale * exact_dot(inverse_zero.T, inner)

    for copy in halos + parts:
        copy.wait_send()
    for copy in outs:
        copy.wait()


def body(band_tiles, band_mask, panels, panel_seed, diag_inverse, cross_block, cross_seed, diag_seed):
    n_col = lax.axis_size("col")
    plane_cols = min(PLANE_COLS, n_col // 2)
    n_a, n_b = 2 * plane_cols, n_col // plane_cols
    part = (WIDE // n_a, TILE)
    scale = 1.0 / math.sqrt(2 * n_col * ROWS * TILE)
    any_spec = pl.BlockSpec(memory_space=pl.ANY)
    vmem = pl.BlockSpec(memory_space=pltpu.VMEM)
    smem = pl.BlockSpec(memory_space=pltpu.SMEM)
    dma = pltpu.SemaphoreType.DMA
    return tuple(
        pl.pallas_call(
            functools.partial(kernel, n_col, plane_cols, scale),
            out_shape=(
                jax.ShapeDtypeStruct(panels.shape, BF16),
                jax.ShapeDtypeStruct((TILE, TILE), F32),
                jax.ShapeDtypeStruct((TILE, TILE), F32),
            ),
            in_specs=[any_spec, smem, any_spec, any_spec, vmem, vmem, vmem, vmem],
            out_specs=(any_spec, vmem, vmem),
            scratch_shapes=[
                pltpu.VMEM((ROWS, BAND + 1, TILE, TILE), BF16),
                pltpu.VMEM((ROWS + BAND, TILE, WIDE), BF16),
                pltpu.VMEM((ROWS, TILE, WIDE), BF16),
                pltpu.VMEM((ROWS, TILE, WIDE), F32),
                pltpu.VMEM((ROWS + BAND, TILE, WIDE), BF16),
                pltpu.VMEM((BAND, TILE, WIDE), BF16),
                pltpu.VMEM((TILE, WIDE), F32),
                pltpu.VMEM((n_a,) + part, BF16),
                pltpu.VMEM((n_a,) + part, BF16),
                pltpu.VMEM((n_b,) + part, BF16),
                pltpu.VMEM((n_a,) + part, BF16),
                pltpu.VMEM(part, BF16),
                pltpu.VMEM((WIDE, WIDE), BF16),
                pltpu.VMEM((WIDE, WIDE), BF16),
                pltpu.VMEM((2, ROWS, TILE, TILE), BF16),
                dma((8,)),
                dma((2,)),
                dma((2,)),
                dma((BAND,)),
                dma((BAND,)),
                dma((3,)),
                dma((3,)),
                dma((2, 2)),
            ],
            compiler_params=pltpu.CompilerParams(
                collective_id=0, has_side_effects=True, vmem_limit_bytes=56 * 1024 * 1024
            ),
        )(band_tiles, band_mask, panels, panel_seed, diag_inverse, cross_block, cross_seed, diag_seed)
    )


def solution(mesh):
    split_rows = P(("col", "row"), None, None, None)
    split_panels = P(None, ("col", "row"), None, None)
    return jax.shard_map(
        body,
        mesh=mesh,
        in_specs=(split_rows, P(("col", "row"), None), split_panels, split_panels, P(), P(), P(), P()),
        out_specs=(split_panels, P(), P()),
        check_vma=False,
    )
```

time: 401 us -> 55.5 us (0.14)
  waiting for transfers between devices: 277 us -> 0 us
  matrix products: 65.6 us -> 0 us
  Pallas kernels: 0 us -> 50.1 us
  local copies, waits for them, and re-layouts: 18.6 us -> 4.56 us
  other arithmetic: 13.7 us -> 0 us
  between operations: 14.3 us -> 0.66 us
  starting transfers between devices: 10.3 us -> 0 us
    psum x1 -> x0, waiting for transfers between devices: 252 us -> none  [body(): cross_total = lax.psum(cross_part, ('col', 'row'))]
    dot_general x16 -> x0, matrix products: 65.6 us -> none  [the longest x5 32.2 us: band_terms(): jnp.einsum('eab,peak->pebk', slot_tiles, below_rows[:, offset:offset + co...]
    pallas_call x0 -> x1, Pallas kernels: none -> 50.1 us  [body(): pl.pallas_call(functools.partial(kernel, n_col, plane_cols, scale), out_s...]
    ppermute x3 -> x0, waiting for transfers between devices: 25.2 us -> none  [the longest x1 25.2 us: padded(): lax.ppermute(tail, axis, [(i, (i + 1) % count) for i in range(ends)])]
    ppermute x3 -> x0, starting transfers between devices: 10.2 us -> none  [the longest x1 4.58 us: passed_along(): return lax.ppermute(shard, axis, pairs)]
    add x1 -> x0, other arithmetic: 5.57 us -> none  [body(): upper_term[:, band_width:]]
    unnamed x31 -> x7, local copies, waits for them, and re-layouts: 10.1 us -> 4.56 us
    slice x3 -> x0, local copies, waits for them, and re-layouts: 4.3 us -> none  [the longest x1 1.66 us: body(): rim_tiles = passed_along(masked[row_count - band_width:], ('col', 'row'), 1)]
  transfers between devices with their start and end apart: 4 -> 0, of which waited for: 2 -> 0; matrix products, arithmetic and copies ran while one was open for 6% -> 0% of each run, Pallas kernels for 0% -> 0%
where the time goes in v1:
time: 55.5 us; the launch traced here: 55.3 us
  Pallas kernels  50.1 us (90%)
  local copies, waits for them, and re-layouts  4.56 us (8%)
  between operations  0.66 us (1%)
    pallas_call x1, Pallas kernels, body(): pl.pallas_call(functools.partial(kernel, n_col, plane_cols, scale), out_s...  50.1 us
    unnamed x7, local copies, waits for them, and re-layouts  4.56 us

profile of v1, /device:TPU:1, one launch (start us, length us, event | category | flops | bytes accessed | tf_op | source)
XLA Modules:
  0.0 55.3 jit_solution(13650137379022369434)
XLA Ops:
  0.6 50.1 %shard_map.103 = (bf16[2,8,256,256]{3,2,1,0:T(8,128)(2,1)}, f32[256,256]{1,0:T(8,128)}, f32[256,256]{1,0:T(8,128)}) custom-call(bf16[8,5,256,256]{3,2,1,0:T(8,128)(2,1)} %band_hbm.1, s32[8,5]{1,0:T(8,128)} %mask.1, bf16[2,8,256,256]{3,2,1,0:T(8,128)(2,1)} %panels_hbm.1, bf16[2,8,256,256]{3,2,1,0:T(8,128)(2,1)} %seed_hbm.1, f32[2,256,256]{2,1,0:T(8,128)} %diag_inverse.1, ...), custom_call_target="tpu_custom_call" | custom-call | tf_op jit(solution)/shard_map/pallas_call | solution.py:341
  50.7 0.0 copy-start.1
  50.7 0.0 copy-start
  50.8 3.2 %copy.14 = bf16[2,8,256,256]{3,2,1,0:T(8,128)(2,1)} copy(bf16[2,8,256,256]{3,2,1,0:T(8,128)(2,1)} %get-tuple-element.6) | data formatting | bytes 4194304
  53.9 0.0 copy-done.1
  53.9 0.7 %copy.15 = f32[256,256]{1,0:T(8,128)} copy(f32[256,256]{1,0:T(8,128)S(1)} %copy-done.1) | data formatting | bytes 524288
  54.6 0.0 copy-done
  54.6 0.7 %copy.16 = f32[256,256]{1,0:T(8,128)} copy(f32[256,256]{1,0:T(8,128)S(1)} %copy-done) | data formatting | bytes 524288
Async XLA Ops:
  50.7 3.2 %copy-start.1 = (f32[256,256]{1,0:T(8,128)S(1)}, f32[256,256]{1,0:T(8,128)}, u32[]{:S(2)}) copy-start(f32[256,256]{1,0:T(8,128)} %get-tuple-element.7) | copy-start | bytes 786436
  50.7 3.9 %copy-start = (f32[256,256]{1,0:T(8,128)S(1)}, f32[256,256]{1,0:T(8,128)}, u32[]{:S(2)}) copy-start(f32[256,256]{1,0:T(8,128)} %get-tuple-element.8) | copy-start | bytes 786436

commit v2 on v1

v2 whole, which is shorter than its diff:
```python
import functools
import math

import jax
import jax.numpy as jnp
from jax import lax
from jax.experimental import pallas as pl
from jax.experimental.pallas import tpu as pltpu
from jax.sharding import PartitionSpec as P

MESH = pl.DeviceIdType.MESH
F32 = jnp.float32
BF16 = jnp.bfloat16
TILE = 256
WIDE = 512
ROWS = 8
BAND = 4
PLANE_COLS = 16


def dot(a, b):
    return jnp.dot(a, b, preferred_element_type=F32)


def dot_t(a, b):
    return lax.dot_general(a, b, (((0,), (0,)), ((), ())), preferred_element_type=F32)


def split(a):
    high = a.astype(BF16)
    return high, (a - high.astype(F32)).astype(BF16)


def dot_three(a, b):
    (a_high, a_low), (b_high, b_low) = split(a), split(b)
    return dot(jnp.concatenate([a_high, a_high, a_low], axis=1), jnp.concatenate([b_high, b_low, b_high], axis=0))


def kernel(
    n_col,
    plane_cols,
    scale,
    band_hbm,
    mask_hbm,
    panels_hbm,
    seed_hbm,
    inverse_hbm,
    cross_hbm,
    cross_seed_hbm,
    diag_seed_hbm,
    out_v,
    cross_out,
    diag_out,
    tiles,
    rows,
    seeds,
    acc,
    resid,
    negm,
    left_in,
    total,
    staged,
    got_a,
    got_b,
    got_c,
    mine,
    w_zero,
    w_one,
    w_last,
    d_zero,
    mask,
    diag_inverse,
    cross_block,
    cross_seed,
    diag_seed,
    in_sem,
    halo_send,
    halo_recv,
    part_send,
    part_recv,
    ar_send,
    ar_recv,
):
    col, row = lax.axis_index("col"), lax.axis_index("row")
    n_dev = 2 * n_col
    index = col * 2 + row
    left, right = lax.rem(index + n_dev - 1, n_dev), lax.rem(index + 1, n_dev)
    left_id = (left // 2, lax.rem(left, 2))
    right_id = (right // 2, lax.rem(right, 2))
    n_a = 2 * plane_cols
    n_b = n_col // plane_cols
    depth, place = col // plane_cols, lax.rem(col, plane_cols)
    me_a = place * 2 + row

    side = math.isqrt(plane_cols) if math.isqrt(plane_cols) ** 2 == plane_cols else 1
    width = plane_cols // side
    moves = [(dx, dy, dc) for dx in range(side) for dy in range(width) for dc in range(2)][1:]
    moves.sort(key=lambda m: -min(m[0], side - m[0]) - min(m[1], width - m[1]))

    def plane_id(move):
        dx, dy, dc = move
        peer_x = lax.rem(place // width + dx, side)
        peer_place = peer_x * width + lax.rem(lax.rem(place, width) + dy, width)
        peer_row = lax.rem(row + dc, 2)
        return peer_place * 2 + peer_row, (depth * plane_cols + peer_place, peer_row)

    line_steps = sorted(range(1, n_b), key=lambda k: -min(k, n_b - k))

    def line_id(step):
        return (lax.rem(depth + step, n_b) * plane_cols + place, row)

    barrier = pltpu.get_barrier_semaphore()
    pl.semaphore_signal(barrier, inc=1, device_id=left_id, device_id_type=MESH)
    pl.semaphore_signal(barrier, inc=1, device_id=right_id, device_id_type=MESH)

    def load(source, target, slot):
        copy = pltpu.make_async_copy(source, target, in_sem.at[slot])
        copy.start()
        return copy

    upper, lower = pl.ds(4, 4), pl.ds(0, 4)
    first, second = pl.ds(0, TILE), pl.ds(TILE, TILE)
    loads_hi = [
        load(mask_hbm, mask, 8),
        load(panels_hbm.at[0, upper], rows.at[upper, :, first], 0),
        load(panels_hbm.at[1, upper], rows.at[upper, :, second], 1),
        load(band_hbm.at[upper], tiles.at[upper], 2),
    ]

    for step in range(1, n_b):
        pl.semaphore_signal(barrier, inc=1, device_id=line_id(step), device_id_type=MESH)
    for move in moves:
        pl.semaphore_signal(barrier, inc=1, device_id=plane_id(move)[1], device_id_type=MESH)

    loads_lo = [
        load(panels_hbm.at[0, lower], rows.at[lower, :, first], 3),
        load(panels_hbm.at[1, lower], rows.at[lower, :, second], 4),
        load(band_hbm.at[lower], tiles.at[lower], 5),
        load(seed_hbm.at[0], seeds.at[:, :, first], 6),
        load(seed_hbm.at[1], seeds.at[:, :, second], 7),
    ]
    loads_last = [
        load(inverse_hbm, diag_inverse, 9),
        load(cross_hbm, cross_block, 10),
        load(cross_seed_hbm, cross_seed, 11),
        load(diag_seed_hbm, diag_seed, 12),
    ]

    def tile(c, d):
        keep = jnp.full((TILE, TILE), mask[c, d].astype(F32), F32).astype(BF16)
        return tiles[c, d] * keep

    def lower_terms(r, slots):
        lhs = jnp.concatenate([tile(r - d, d) for d in slots], axis=1)
        rhs = rows[pl.ds(r - slots[0], len(slots))].reshape(len(slots) * TILE, WIDE)
        return dot(lhs, rhs)

    def upper_terms(i, slots):
        lhs = jnp.concatenate([tile(i, d) for d in slots], axis=0)
        rhs = rows[pl.ds(i + slots[0], len(slots))].reshape(len(slots) * TILE, WIDE)
        return dot_t(lhs, rhs)

    halos = []
    for begin in (0, 2):
        for p, lanes in ((0, first), (1, second)):
            halos.append(
                pltpu.make_async_remote_copy(
                    src_ref=panels_hbm.at[p, pl.ds(begin, 2)],
                    dst_ref=rows.at[pl.ds(8 + begin, 2), :, lanes],
                    send_sem=halo_send.at[p, begin // 2],
                    recv_sem=halo_recv.at[p, begin // 2],
                    device_id=left_id,
                    device_id_type=MESH,
                )
            )
    parts = []
    for begin in (2, 0):
        parts.append(
            pltpu.make_async_remote_copy(
                src_ref=resid.at[pl.ds(8 + begin, 2)],
                dst_ref=left_in.at[pl.ds(begin, 2)],
                send_sem=part_send.at[begin // 2],
                recv_sem=part_recv.at[begin // 2],
                device_id=right_id,
                device_id_type=MESH,
            )
        )

    pl.semaphore_wait(barrier, n_a + n_b)
    halos[0].start()
    halos[1].start()

    for copy in loads_hi:
        copy.wait()
    for r in (11, 10):
        resid[r] = (-lower_terms(r, list(range(4, r - 8, -1)))).astype(BF16)
    parts[0].start()
    for r in (9, 8):
        resid[r] = (-lower_terms(r, list(range(4, r - 8, -1)))).astype(BF16)

    def own_terms(i, slots):
        value = seeds[i].astype(F32)
        turned = -dot(tile(i, 0), rows[i, :, :TILE])
        if slots:
            terms = lower_terms(i, slots)
            value = value - terms
            turned = turned - terms[:, :TILE]
        acc[i] = value
        resid[i] = value.astype(BF16)
        negm[i] = turned.astype(BF16)

    def sum_over(i):
        lhs = jnp.concatenate([rows[i, :, :TILE], negm[i]], axis=0)
        rhs = jnp.concatenate([resid[i], rows[i]], axis=0)
        return dot_t(lhs, rhs)

    for copy in loads_lo:
        copy.wait()
    total[...] = jnp.zeros_like(total)

    @pl.loop(4, 8)
    def _(i):
        own_terms(i, [4, 3, 2, 1])
        total[...] += sum_over(i)

    for i in range(4):
        own_terms(i, list(range(i, 0, -1)))

    @pl.loop(0, 2)
    def _(i):
        total[...] += sum_over(i)

    parts[0].wait_recv()
    for i in (2, 3):
        arrived = left_in[i].astype(F32)
        value = acc[i] + arrived
        acc[i] = value
        resid[i] = value.astype(BF16)
        negm[i] = (negm[i].astype(F32) + arrived[:, :TILE]).astype(BF16)

    @pl.loop(2, 4)
    def _(i):
        total[...] += sum_over(i)

    halos[0].wait_recv()
    halos[1].wait_recv()
    for i in (8, 9):
        lhs = jnp.concatenate([rows[i, :, :TILE], resid[i, :, :TILE]], axis=0)
        rhs = jnp.concatenate([resid[i], rows[i]], axis=0)
        total[...] += dot_t(lhs, rhs)

    part_rows = WIDE // n_a
    for p in range(2):
        half = total[:, p * TILE : (p + 1) * TILE].astype(BF16)
        staged[pl.ds(p * n_a // 2, n_a // 2)] = half.reshape(n_a // 2, part_rows, TILE)

    for move in moves:
        peer, peer_id = plane_id(move)
        pltpu.make_async_remote_copy(
            src_ref=staged.at[peer],
            dst_ref=got_a.at[me_a],
            send_sem=ar_send.at[0],
            recv_sem=ar_recv.at[0],
            device_id=peer_id,
            device_id_type=MESH,
        ).start()

    halos[2].start()
    halos[3].start()
    parts[1].start()
    got_a[me_a] = staged[me_a]

    def wait_bytes(buffer, count, send, recv):
        view = buffer.at[pl.ds(0, count)]
        pltpu.make_async_copy(view, view, recv).wait()
        pltpu.make_async_copy(view, view, send).wait()

    for copy in loads_last:
        copy.wait()

    zero_high, zero_low = split(diag_inverse[0])
    one_high, one_low = split(diag_inverse[1])
    cross = cross_block[...]
    crosses = jnp.concatenate([cross, cross], axis=0)
    through = dot(jnp.concatenate([one_high, one_low], axis=1), crosses)
    through_high, through_low = split(through)
    carry_high, carry_low = split(-dot_three(through, diag_inverse[0]))
    w_zero[...] = jnp.concatenate([zero_high, carry_high, zero_low, carry_low], axis=0)
    w_one[...] = jnp.concatenate([one_high, one_low], axis=0)
    w_last[:TILE] = jnp.concatenate([one_high, through_high], axis=1)
    w_last[TILE:] = jnp.concatenate([one_low, through_low], axis=1)
    d_zero[...] = jnp.concatenate([zero_high, zero_low, zero_high], axis=0)
    base = dot_three(cross_seed[...], diag_inverse[0])
    cross_out[...] = base
    diag_out[...] = diag_seed[...] - dot_t(jnp.concatenate(split(base), axis=0), crosses)

    @pl.loop(0, 4)
    def _(i):
        acc[i] = acc[i] - upper_terms(i, [0, 1, 2, 3, 4])

    def solve(begin):
        value = resid[pl.ds(begin, 2)].reshape(2 * TILE, WIDE)
        one = value[:, TILE:]
        zero_term = dot(jnp.concatenate([value, value], axis=1), w_zero[...])
        one_term = dot(jnp.concatenate([one, one], axis=1), w_one[...])
        for p, term in ((0, zero_term), (1, one_term)):
            out_v[p, pl.ds(begin, 2)] = term.astype(BF16).reshape(2, TILE, TILE)

    resid[pl.ds(2, 2)] = acc[pl.ds(2, 2)].astype(BF16)
    solve(2)

    wait_bytes(got_a, n_a - 1, ar_send.at[0], ar_recv.at[0])
    mine[...] = jnp.sum(got_a[...].astype(F32), axis=0).astype(BF16)

    for step in line_steps:
        pltpu.make_async_remote_copy(
            src_ref=mine,
            dst_ref=got_b.at[depth],
            send_sem=ar_send.at[1],
            recv_sem=ar_recv.at[1],
            device_id=line_id(step),
            device_id_type=MESH,
        ).start()

    got_b[depth] = mine[...]

    @pl.loop(4, 6)
    def _(i):
        resid[i] = (acc[i] - upper_terms(i, [0, 1, 2, 3, 4])).astype(BF16)

    solve(4)
    acc[6] = acc[6] - upper_terms(6, [0, 1, 2, 3])
    acc[7] = acc[7] - upper_terms(7, [0, 1, 2])

    wait_bytes(got_b, n_b - 1, ar_send.at[1], ar_recv.at[1])
    got_c[me_a] = jnp.sum(got_b[...].astype(F32), axis=0).astype(BF16)

    for move in moves:
        pltpu.make_async_remote_copy(
            src_ref=got_c.at[me_a],
            dst_ref=got_c.at[me_a],
            send_sem=ar_send.at[2],
            recv_sem=ar_recv.at[2],
            device_id=plane_id(move)[1],
            device_id_type=MESH,
        ).start()

    parts[1].wait_recv()
    resid[pl.ds(0, 2)] = (acc[pl.ds(0, 2)] + left_in[pl.ds(0, 2)].astype(F32)).astype(BF16)
    solve(0)
    halos[2].wait_recv()
    halos[3].wait_recv()
    resid[6] = (acc[6] - upper_terms(6, [4])).astype(BF16)
    resid[7] = (acc[7] - upper_terms(7, [3, 4])).astype(BF16)
    solve(6)

    wait_bytes(got_c, n_a - 1, ar_send.at[2], ar_recv.at[2])
    zero_sum = got_c[pl.ds(0, n_a // 2)].reshape(TILE, TILE)
    one_sum = got_c[pl.ds(n_a // 2, n_a // 2)].reshape(TILE, TILE)
    mixed = dot(jnp.concatenate([one_sum, one_sum], axis=1), w_last[...])
    high, low = split(mixed[:, :TILE].T)
    cross_out[...] -= scale * dot(jnp.concatenate([high, high, low], axis=1), d_zero[...])
    mixed = mixed[:, TILE:]
    high, low = split(mixed + (mixed - zero_sum.astype(F32)).T)
    diag_out[...] += scale * dot_t(d_zero[...], jnp.concatenate([high, high, low], axis=0))

    for copy in halos + parts:
        copy.wait_send()


def body(band_tiles, band_mask, panels, panel_seed, diag_inverse, cross_block, cross_seed, diag_seed):
    n_col = lax.axis_size("col")
    plane_cols = min(PLANE_COLS, n_col // 2)
    n_a, n_b = 2 * plane_cols, n_col // plane_cols
    part = (WIDE // n_a, TILE)
    scale = 1.0 / math.sqrt(2 * n_col * ROWS * TILE)
    arrays = (band_tiles, band_mask, panels, panel_seed, diag_inverse, cross_block, cross_seed, diag_seed)
    any_spec = pl.BlockSpec(memory_space=pltpu.HBM)
    vmem = pl.BlockSpec(memory_space=pltpu.VMEM)
    dma = pltpu.SemaphoreType.DMA
    return tuple(
        pl.pallas_call(
            functools.partial(kernel, n_col, plane_cols, scale),
            out_shape=(
                pltpu.VMEM(panels.shape, BF16),
                pltpu.VMEM((TILE, TILE), F32),
                pltpu.VMEM((TILE, TILE), F32),
            ),
            in_specs=[any_spec] * 8,
            out_specs=(vmem, vmem, vmem),
            scratch_shapes=[
                pltpu.VMEM((ROWS, BAND + 1, TILE, TILE), BF16),
                pltpu.VMEM((ROWS + BAND, TILE, WIDE), BF16),
                pltpu.VMEM((ROWS, TILE, WIDE), BF16),
                pltpu.VMEM((ROWS, TILE, WIDE), F32),
                pltpu.VMEM((ROWS + BAND, TILE, WIDE), BF16),
                pltpu.VMEM((ROWS, TILE, TILE), BF16),
                pltpu.VMEM((BAND, TILE, WIDE), BF16),
                pltpu.VMEM((TILE, WIDE), F32),
                pltpu.VMEM((n_a,) + part, BF16),
                pltpu.VMEM((n_a,) + part, BF16),
                pltpu.VMEM((n_b,) + part, BF16),
                pltpu.VMEM((n_a,) + part, BF16),
                pltpu.VMEM(part, BF16),
                pltpu.VMEM((4 * TILE, TILE), BF16),
                pltpu.VMEM((2 * TILE, TILE), BF16),
                pltpu.VMEM((2 * TILE, WIDE), BF16),
                pltpu.VMEM((3 * TILE, TILE), BF16),
                pltpu.SMEM((ROWS, BAND + 1), jnp.int32),
                pltpu.VMEM((2, TILE, TILE), F32),
                pltpu.VMEM((TILE, TILE), BF16),
                pltpu.VMEM((TILE, TILE), F32),
                pltpu.VMEM((TILE, TILE), F32),
                dma((13,)),
                dma((2, 2)),
                dma((2, 2)),
                dma((2,)),
                dma((2,)),
                dma((3,)),
                dma((3,)),
            ],
            compiler_params=pltpu.CompilerParams(
                collective_id=0, has_side_effects=True, vmem_limit_bytes=40 * 1024 * 1024
            ),
        )(*(pltpu.with_memory_space_constraint(array, pltpu.HBM) for array in arrays))
    )


def solution(mesh):
    split_rows = P(("col", "row"), None, None, None)
    split_panels = P(None, ("col", "row"), None, None)
    return jax.shard_map(
        body,
        mesh=mesh,
        in_specs=(split_rows, P(("col", "row"), None), split_panels, split_panels, P(), P(), P(), P()),
        out_specs=(split_panels, P(), P()),
        check_vma=False,
    )
```

time: 55.5 us -> 44.8 us (0.81)
  Pallas kernels: 50.1 us -> 41.3 us
  local copies, waits for them, and re-layouts: 4.56 us -> 2.73 us
    pallas_call x1, Pallas kernels: 50.1 us -> 41.3 us  [body(): pl.pallas_call(functools.partial(kernel, n_col, plane_cols, scale), out_s...]
    unnamed x7 -> x3, local copies, waits for them, and re-layouts: 4.56 us -> 2.73 us
where the time goes in v2:
time: 44.8 us; the launch traced here: 44.7 us
  Pallas kernels  41.3 us (92%)
  local copies, waits for them, and re-layouts  2.73 us (6%)
  between operations  0.64 us (1%)
    pallas_call x1, Pallas kernels, body(): pl.pallas_call(functools.partial(kernel, n_col, plane_cols, scale), out_s...  41.3 us
    unnamed x3, local copies, waits for them, and re-layouts  2.73 us

profile of v2, /device:TPU:1, one launch (start us, length us, event | category | flops | bytes accessed | tf_op | source)
XLA Modules:
  0.0 44.7 jit_solution(12061613161186885670)
XLA Ops:
  0.6 41.3 %shard_map.103 = (bf16[2,8,256,256]{3,2,1,0:T(8,128)(2,1)S(1)}, f32[256,256]{1,0:T(8,128)S(1)}, f32[256,256]{1,0:T(8,128)S(1)}) custom-call(bf16[8,5,256,256]{3,2,1,0:T(8,128)(2,1)} %band_hbm.1, s32[8,5]{1,0:T(8,128)} %mask_hbm.1, bf16[2,8,256,256]{3,2,1,0:T(8,128)(2,1)} %panels_hbm.1, bf16[2,8,256,256]{3,2,1,0:T(8,128)(2,1)} %seed_hbm.1, ...), custom_call_target="tpu_custom_call" | custom-call | tf_op jit(solution)/shard_map/pallas_call | solution.py:382
  42.0 1.3 %copy.14 = bf16[2,8,256,256]{3,2,1,0:T(8,128)(2,1)} copy(bf16[2,8,256,256]{3,2,1,0:T(8,128)(2,1)S(1)} %get-tuple-element.3) | data formatting | bytes 4194304
  43.3 0.7 %copy.15 = f32[256,256]{1,0:T(8,128)} copy(f32[256,256]{1,0:T(8,128)S(1)} %get-tuple-element.4) | data formatting | bytes 524288
  44.0 0.7 %copy.16 = f32[256,256]{1,0:T(8,128)} copy(f32[256,256]{1,0:T(8,128)S(1)} %get-tuple-element.5) | data formatting | bytes 524288

commit v3 on v2

--- a/solution.py
+++ b/solution.py
@@ -39,7 +39,6 @@
 def kernel(
     n_col,
     plane_cols,
-    scale,
     band_hbm,
     mask_hbm,
     panels_hbm,
@@ -49,8 +48,11 @@
     cross_seed_hbm,
     diag_seed_hbm,
     out_v,
-    cross_out,
-    diag_out,
+    sums,
+    w_last,
+    d_zero,
+    cross_base,
+    diag_base,
     tiles,
     rows,
     seeds,
@@ -66,8 +68,6 @@
     mine,
     w_zero,
     w_one,
-    w_last,
-    d_zero,
     mask,
     diag_inverse,
     cross_block,
@@ -175,16 +175,17 @@
             )
     parts = []
     for begin in (2, 0):
-        parts.append(
-            pltpu.make_async_remote_copy(
-                src_ref=resid.at[pl.ds(8 + begin, 2)],
-                dst_ref=left_in.at[pl.ds(begin, 2)],
-                send_sem=part_send.at[begin // 2],
-                recv_sem=part_recv.at[begin // 2],
-                device_id=right_id,
-                device_id_type=MESH,
+        for p, lanes in ((0, first), (1, second)):
+            parts.append(
+                pltpu.make_async_remote_copy(
+                    src_ref=resid.at[pl.ds(8 + begin, 2), :, lanes],
+                    dst_ref=left_in.at[pl.ds(begin, 2), :, lanes],
+                    send_sem=part_send.at[p, begin // 2],
+                    recv_sem=part_recv.at[p, begin // 2],
+                    device_id=right_id,
+                    device_id_type=MESH,
+                )
             )
-        )
 
     pl.semaphore_wait(barrier, n_a + n_b)
     halos[0].start()
@@ -195,6 +196,7 @@
     for r in (11, 10):
         resid[r] = (-lower_terms(r, list(range(4, r - 8, -1)))).astype(BF16)
     parts[0].start()
+    parts[1].start()
     for r in (9, 8):
         resid[r] = (-lower_terms(r, list(range(4, r - 8, -1)))).astype(BF16)
 
@@ -230,51 +232,80 @@
     def _(i):
         total[...] += sum_over(i)
 
-    parts[0].wait_recv()
-    for i in (2, 3):
-        arrived = left_in[i].astype(F32)
-        value = acc[i] + arrived
-        acc[i] = value
-        resid[i] = value.astype(BF16)
-        negm[i] = (negm[i].astype(F32) + arrived[:, :TILE]).astype(BF16)
-
-    @pl.loop(2, 4)
-    def _(i):
-        total[...] += sum_over(i)
-
-    halos[0].wait_recv()
-    halos[1].wait_recv()
-    for i in (8, 9):
-        lhs = jnp.concatenate([rows[i, :, :TILE], resid[i, :, :TILE]], axis=0)
-        rhs = jnp.concatenate([resid[i], rows[i]], axis=0)
-        total[...] += dot_t(lhs, rhs)
-
-    part_rows = WIDE // n_a
+    edge = (2, 3)
+    beyond = (8, 9)
+    part_rows = 2 * TILE // n_a
+    half = n_a // 2
+
+    def wait_bytes(buffer, count, stage, p):
+        view = buffer.at[p, pl.ds(0, count)]
+        pltpu.make_async_copy(view, view, ar_recv.at[stage, p]).wait()
+        pltpu.make_async_copy(view, view, ar_send.at[stage, p]).wait()
+
+    def scatter(p):
+        for move in moves:
+            peer, peer_id = plane_id(move)
+            pltpu.make_async_remote_copy(
+                src_ref=staged.at[p, peer],
+                dst_ref=got_a.at[p, me_a],
+                send_sem=ar_send.at[0, p],
+                recv_sem=ar_recv.at[0, p],
+                device_id=peer_id,
+                device_id_type=MESH,
+            ).start()
+        got_a[p, me_a] = staged[p, me_a]
+
+    def across(p):
+        wait_bytes(got_a, n_a - 1, 0, p)
+        mine[p] = jnp.sum(got_a[p].astype(F32), axis=0).astype(BF16)
+        for step in line_steps:
+            pltpu.make_async_remote_copy(
+                src_ref=mine.at[p],
+                dst_ref=got_b.at[p, depth],
+                send_sem=ar_send.at[1, p],
+                recv_sem=ar_recv.at[1, p],
+                device_id=line_id(step),
+                device_id_type=MESH,
+            ).start()
+        got_b[p, depth] = mine[p]
+
+    def gather(p):
+        wait_bytes(got_b, n_b - 1, 1, p)
+        got_c[p, me_a] = jnp.sum(got_b[p].astype(F32), axis=0).astype(BF16)
+        for move in moves:
+            pltpu.make_async_remote_copy(
+                src_ref=got_c.at[p, me_a],
+                dst_ref=got_c.at[p, me_a],
+                send_sem=ar_send.at[2, p],
+                recv_sem=ar_recv.at[2, p],
+                device_id=plane_id(move)[1],
+                device_id_type=MESH,
+            ).start()
+
     for p in range(2):
-        half = total[:, p * TILE : (p + 1) * TILE].astype(BF16)
-        staged[pl.ds(p * n_a // 2, n_a // 2)] = half.reshape(n_a // 2, part_rows, TILE)
-
-    for move in moves:
-        peer, peer_id = plane_id(move)
-        pltpu.make_async_remote_copy(
-            src_ref=staged.at[peer],
-            dst_ref=got_a.at[me_a],
-            send_sem=ar_send.at[0],
-            recv_sem=ar_recv.at[0],
-            device_id=peer_id,
-            device_id_type=MESH,
-        ).start()
-
-    halos[2].start()
-    halos[3].start()
-    parts[1].start()
-    got_a[me_a] = staged[me_a]
-
-    def wait_bytes(buffer, count, send, recv):
-        view = buffer.at[pl.ds(0, count)]
-        pltpu.make_async_copy(view, view, recv).wait()
-        pltpu.make_async_copy(view, view, send).wait()
-
+        begin = p * TILE
+        parts[p].wait_recv()
+        for i in edge:
+            arrived = left_in[i, :, begin : begin + TILE].astype(F32)
+            value = acc[i, :, begin : begin + TILE] + arrived
+            acc[i, :, begin : begin + TILE] = value
+            resid[i, :, begin : begin + TILE] = value.astype(BF16)
+            if p == 0:
+                negm[i] = (negm[i].astype(F32) + arrived).astype(BF16)
+        halos[p].wait_recv()
+        lhs = [rows[i, :, :TILE] for i in edge + beyond] + [negm[i] for i in edge]
+        lhs += [resid[i, :, :TILE] for i in beyond]
+        rhs = [resid[i, :, begin : begin + TILE] for i in edge + beyond]
+        rhs += [rows[i, :, begin : begin + TILE] for i in edge + beyond]
+        value = total[:, begin : begin + TILE]
+        value = value + dot_t(jnp.concatenate(lhs, axis=0), jnp.concatenate(rhs, axis=0))
+        value = value.astype(BF16)
+        for k in range(2):
+            staged[p, pl.ds(k * half, half)] = value[:, k * 128 : (k + 1) * 128].reshape(half, part_rows, 128)
+        scatter(p)
+
+    for copy in halos[2:] + parts[2:]:
+        copy.start()
     for copy in loads_last:
         copy.wait()
 
@@ -291,8 +322,8 @@
     w_last[TILE:] = jnp.concatenate([one_low, through_low], axis=1)
     d_zero[...] = jnp.concatenate([zero_high, zero_low, zero_high], axis=0)
     base = dot_three(cross_seed[...], diag_inverse[0])
-    cross_out[...] = base
-    diag_out[...] = diag_seed[...] - dot_t(jnp.concatenate(split(base), axis=0), crosses)
+    cross_base[...] = base
+    diag_base[...] = diag_seed[...] - dot_t(jnp.concatenate(split(base), axis=0), crosses)
 
     @pl.loop(0, 4)
     def _(i):
@@ -306,123 +337,145 @@
         for p, term in ((0, zero_term), (1, one_term)):
             out_v[p, pl.ds(begin, 2)] = term.astype(BF16).reshape(2, TILE, TILE)
 
+    across(0)
+
     resid[pl.ds(2, 2)] = acc[pl.ds(2, 2)].astype(BF16)
     solve(2)
-
-    wait_bytes(got_a, n_a - 1, ar_send.at[0], ar_recv.at[0])
-    mine[...] = jnp.sum(got_a[...].astype(F32), axis=0).astype(BF16)
-
-    for step in line_steps:
-        pltpu.make_async_remote_copy(
-            src_ref=mine,
-            dst_ref=got_b.at[depth],
-            send_sem=ar_send.at[1],
-            recv_sem=ar_recv.at[1],
-            device_id=line_id(step),
-            device_id_type=MESH,
-        ).start()
-
-    got_b[depth] = mine[...]
+    across(1)
 
     @pl.loop(4, 6)
     def _(i):
         resid[i] = (acc[i] - upper_terms(i, [0, 1, 2, 3, 4])).astype(BF16)
 
-    solve(4)
     acc[6] = acc[6] - upper_terms(6, [0, 1, 2, 3])
     acc[7] = acc[7] - upper_terms(7, [0, 1, 2])
-
-    wait_bytes(got_b, n_b - 1, ar_send.at[1], ar_recv.at[1])
-    got_c[me_a] = jnp.sum(got_b[...].astype(F32), axis=0).astype(BF16)
-
-    for move in moves:
-        pltpu.make_async_remote_copy(
-            src_ref=got_c.at[me_a],
-            dst_ref=got_c.at[me_a],
-            send_sem=ar_send.at[2],
-            recv_sem=ar_recv.at[2],
-            device_id=plane_id(move)[1],
-            device_id_type=MESH,
-        ).start()
-
-    parts[1].wait_recv()
+    gather(0)
+
+    solve(4)
+    gather(1)
+
+    for copy in parts[2:] + halos[2:]:
+        copy.wait_recv()
     resid[pl.ds(0, 2)] = (acc[pl.ds(0, 2)] + left_in[pl.ds(0, 2)].astype(F32)).astype(BF16)
     solve(0)
-    halos[2].wait_recv()
-    halos[3].wait_recv()
     resid[6] = (acc[6] - upper_terms(6, [4])).astype(BF16)
     resid[7] = (acc[7] - upper_terms(7, [3, 4])).astype(BF16)
     solve(6)
-
-    wait_bytes(got_c, n_a - 1, ar_send.at[2], ar_recv.at[2])
-    zero_sum = got_c[pl.ds(0, n_a // 2)].reshape(TILE, TILE)
-    one_sum = got_c[pl.ds(n_a // 2, n_a // 2)].reshape(TILE, TILE)
+    for copy in halos + parts:
+        copy.wait_send()
+
+    for p in range(2):
+        wait_bytes(got_c, n_a - 1, 2, p)
+        for k in range(2):
+            sums[p, :, k * 128 : (k + 1) * 128] = got_c[p, pl.ds(k * half, half)].reshape(TILE, 128)
+
+
+def finish(
+    scale,
+    out_v,
+    sums,
+    w_last,
+    d_zero,
+    cross_base,
+    diag_base,
+    out_hbm,
+    cross_hbm,
+    diag_hbm,
+    cross_v,
+    diag_v,
+    sem,
+):
+    copies = [
+        pltpu.make_async_copy(out_v, out_hbm, sem.at[0]),
+        pltpu.make_async_copy(cross_v, cross_hbm, sem.at[1]),
+        pltpu.make_async_copy(diag_v, diag_hbm, sem.at[2]),
+    ]
+    copies[0].start()
+    one_sum = sums[1]
     mixed = dot(jnp.concatenate([one_sum, one_sum], axis=1), w_last[...])
     high, low = split(mixed[:, :TILE].T)
-    cross_out[...] -= scale * dot(jnp.concatenate([high, high, low], axis=1), d_zero[...])
+    cross_v[...] = cross_base[...] - scale * dot(jnp.concatenate([high, high, low], axis=1), d_zero[...])
+    copies[1].start()
     mixed = mixed[:, TILE:]
-    high, low = split(mixed + (mixed - zero_sum.astype(F32)).T)
-    diag_out[...] += scale * dot_t(d_zero[...], jnp.concatenate([high, high, low], axis=0))
-
-    for copy in halos + parts:
-        copy.wait_send()
+    high, low = split(mixed + (mixed - sums[0].astype(F32)).T)
+    diag_v[...] = diag_base[...] + scale * dot_t(d_zero[...], jnp.concatenate([high, high, low], axis=0))
+    copies[2].start()
+    for copy in copies:
+        copy.wait()
 
 
 def body(band_tiles, band_mask, panels, panel_seed, diag_inverse, cross_block, cross_seed, diag_seed):
     n_col = lax.axis_size("col")
     plane_cols = min(PLANE_COLS, n_col // 2)
     n_a, n_b = 2 * plane_cols, n_col // plane_cols
-    part = (WIDE // n_a, TILE)
+    part = (2 * TILE // n_a, 128)
     scale = 1.0 / math.sqrt(2 * n_col * ROWS * TILE)
     arrays = (band_tiles, band_mask, panels, panel_seed, diag_inverse, cross_block, cross_seed, diag_seed)
     any_spec = pl.BlockSpec(memory_space=pltpu.HBM)
     vmem = pl.BlockSpec(memory_space=pltpu.VMEM)
     dma = pltpu.SemaphoreType.DMA
+    held = pl.pallas_call(
+        functools.partial(kernel, n_col, plane_cols),
+        out_shape=(
+            pltpu.VMEM(panels.shape, BF16),
+            pltpu.VMEM((2, TILE, TILE), BF16),
+            pltpu.VMEM((2 * TILE, WIDE), BF16),
+            pltpu.VMEM((3 * TILE, TILE), BF16),
+            pltpu.VMEM((TILE, TILE), F32),
+            pltpu.VMEM((TILE, TILE), F32),
+        ),
+        in_specs=[any_spec] * 8,
+        out_specs=(vmem,) * 6,
+        scratch_shapes=[
+            pltpu.VMEM((ROWS, BAND + 1, TILE, TILE), BF16),
+            pltpu.VMEM((ROWS + BAND, TILE, WIDE), BF16),
+            pltpu.VMEM((ROWS, TILE, WIDE), BF16),
+            pltpu.VMEM((ROWS, TILE, WIDE), F32),
+            pltpu.VMEM((ROWS + BAND, TILE, WIDE), BF16),
+            pltpu.VMEM((ROWS, TILE, TILE), BF16),
+            pltpu.VMEM((BAND, TILE, WIDE), BF16),
+            pltpu.VMEM((TILE, WIDE), F32),
+            pltpu.VMEM((2, n_a) + part, BF16),
+            pltpu.VMEM((2, n_a) + part, BF16),
+            pltpu.VMEM((2, n_b) + part, BF16),
+            pltpu.VMEM((2, n_a) + part, BF16),
+            pltpu.VMEM((2,) + part, BF16),
+            pltpu.VMEM((4 * TILE, TILE), BF16),
+            pltpu.VMEM((2 * TILE, TILE), BF16),
+            pltpu.SMEM((ROWS, BAND + 1), jnp.int32),
+            pltpu.VMEM((2, TILE, TILE), F32),
+            pltpu.VMEM((TILE, TILE), BF16),
+            pltpu.VMEM((TILE, TILE), F32),
+            pltpu.VMEM((TILE, TILE), F32),
+            dma((13,)),
+            dma((2, 2)),
+            dma((2, 2)),
+            dma((2, 2)),
+            dma((2, 2)),
+            dma((3, 2)),
+            dma((3, 2)),
+        ],
+        compiler_params=pltpu.CompilerParams(
+            collective_id=0, has_side_effects=True, vmem_limit_bytes=40 * 1024 * 1024
+        ),
+    )(*(pltpu.with_memory_space_constraint(array, pltpu.HBM) for array in arrays))
     return tuple(
         pl.pallas_call(
-            functools.partial(kernel, n_col, plane_cols, scale),
+            functools.partial(finish, scale),
             out_shape=(
-                pltpu.VMEM(panels.shape, BF16),
+                jax.ShapeDtypeStruct(panels.shape, BF16),
+                jax.ShapeDtypeStruct((TILE, TILE), F32),
+                jax.ShapeDtypeStruct((TILE, TILE), F32),
+            ),
+            in_specs=[vmem] * 6,
+            out_specs=(pl.BlockSpec(memory_space=pl.ANY),) * 3,
+            scratch_shapes=[
                 pltpu.VMEM((TILE, TILE), F32),
                 pltpu.VMEM((TILE, TILE), F32),
-            ),
-            in_specs=[any_spec] * 8,
-            out_specs=(vmem, vmem, vmem),
-            scratch_shapes=[
-                pltpu.VMEM((ROWS, BAND + 1, TILE, TILE), BF16),
-                pltpu.VMEM((ROWS + BAND, TILE, WIDE), BF16),
-                pltpu.VMEM((ROWS, TILE, WIDE), BF16),
-                pltpu.VMEM((ROWS, TILE, WIDE), F32),
-                pltpu.VMEM((ROWS + BAND, TILE, WIDE), BF16),
-                pltpu.VMEM((ROWS, TILE, TILE), BF16),
-                pltpu.VMEM((BAND, TILE, WIDE), BF16),
-                pltpu.VMEM((TILE, WIDE), F32),
-                pltpu.VMEM((n_a,) + part, BF16),
-                pltpu.VMEM((n_a,) + part, BF16),
-                pltpu.VMEM((n_b,) + part, BF16),
-                pltpu.VMEM((n_a,) + part, BF16),
-                pltpu.VMEM(part, BF16),
-                pltpu.VMEM((4 * TILE, TILE), BF16),
-                pltpu.VMEM((2 * TILE, TILE), BF16),
-                pltpu.VMEM((2 * TILE, WIDE), BF16),
-                pltpu.VMEM((3 * TILE, TILE), BF16),
-                pltpu.SMEM((ROWS, BAND + 1), jnp.int32),
-                pltpu.VMEM((2, TILE, TILE), F32),
-                pltpu.VMEM((TILE, TILE), BF16),
-                pltpu.VMEM((TILE, TILE), F32),
-                pltpu.VMEM((TILE, TILE), F32),
-                dma((13,)),
-                dma((2, 2)),
-                dma((2, 2)),
-                dma((2,)),
-                dma((2,)),
-                dma((3,)),
                 dma((3,)),
             ],
-            compiler_params=pltpu.CompilerParams(
-                collective_id=0, has_side_effects=True, vmem_limit_bytes=40 * 1024 * 1024
-            ),
-        )(*(pltpu.with_memory_space_constraint(array, pltpu.HBM) for array in arrays))
+            compiler_params=pltpu.CompilerParams(vmem_limit_bytes=16 * 1024 * 1024),
+        )(*(pltpu.with_memory_space_constraint(array, pltpu.VMEM) for array in held))
     )
 
 

time: 44.8 us -> 41.4 us (0.924)
  local copies, waits for them, and re-layouts: 2.73 us -> 0 us
  Pallas kernels: 41.3 us -> 40.7 us
    unnamed x3 -> x0, local copies, waits for them, and re-layouts: 2.73 us -> none
    pallas_call x1 -> x2, Pallas kernels: 41.3 us -> 40.7 us  [the longest x1 39.1 us: body(): pl.pallas_call(functools.partial(kernel, n_col, plane_cols), out_shape=(p...]
where the time goes in v3:
time: 41.4 us; the launch traced here: 41.3 us
  Pallas kernels  40.7 us (98%)
  between operations  0.64 us (2%)
    pallas_call x1, Pallas kernels, body(): pl.pallas_call(functools.partial(kernel, n_col, plane_cols), out_shape=(p...  39.1 us
    pallas_call x1, Pallas kernels, body(): pl.pallas_call(functools.partial(finish, scale), out_shape=(jax.ShapeDtyp...  1.58 us

profile of v3, /device:TPU:1, one launch (start us, length us, event | category | flops | bytes accessed | tf_op | source)
XLA Modules:
  0.0 41.3 jit_solution(16015409729405609663)
XLA Ops:
  0.6 39.1 %shard_map.103 = (bf16[2,8,256,256]{3,2,1,0:T(8,128)(2,1)S(1)}, bf16[2,256,256]{2,1,0:T(8,128)(2,1)S(1)}, bf16[512,512]{1,0:T(8,128)(2,1)S(1)}, bf16[768,256]{1,...) custom-call(bf16[8,5,256,256]{3,2,1,0:T(8,128)(2,1)} %band_hbm.1, s32[8,5]{1,0:T(8,128)} %mask_hbm.1, ...), custom_call_target="tpu_custom_call" | custom-call | tf_op jit(solution)/shard_map/pallas_call | solution.py:417
  39.7 1.6 %shard_map.104 = (bf16[2,8,256,256]{3,2,1,0:T(8,128)(2,1)}, f32[256,256]{1,0:T(8,128)}, f32[256,256]{1,0:T(8,128)}) custom-call(bf16[2,8,256,256]{3,2,1,0:T(8,128)(2,1)S(1)} %get-tuple-element.9.out_v, bf16[2,256,256]{2,1,0:T(8,128)(2,1)S(1)} %get-tuple-element.10.sums, bf16[512,512]{1,0:T(8,128)(2,1)S(1)} %get-tuple-element.11.w_last, ...), custom_call_target="tpu_custom_call" | custom-call | tf_op jit(solution)/shard_map/pallas_call | solution.py:463

commit v4 on v3

--- a/solution.py
+++ b/solution.py
@@ -118,32 +118,37 @@
         copy.start()
         return copy
 
-    upper, lower = pl.ds(4, 4), pl.ds(0, 4)
+    lower, edge_rows, middle = pl.ds(0, 4), pl.ds(6, 2), pl.ds(4, 2)
     first, second = pl.ds(0, TILE), pl.ds(TILE, TILE)
-    loads_hi = [
-        load(mask_hbm, mask, 8),
-        load(panels_hbm.at[0, upper], rows.at[upper, :, first], 0),
-        load(panels_hbm.at[1, upper], rows.at[upper, :, second], 1),
-        load(band_hbm.at[upper], tiles.at[upper], 2),
+    loads_edge = [
+        load(mask_hbm, mask, 0),
+        load(band_hbm.at[edge_rows], tiles.at[edge_rows], 1),
+        load(panels_hbm.at[0, edge_rows], rows.at[edge_rows, :, first], 2),
+        load(panels_hbm.at[1, edge_rows], rows.at[edge_rows, :, second], 3),
     ]
 
-    for step in range(1, n_b):
+    for step in line_steps:
         pl.semaphore_signal(barrier, inc=1, device_id=line_id(step), device_id_type=MESH)
     for move in moves:
         pl.semaphore_signal(barrier, inc=1, device_id=plane_id(move)[1], device_id_type=MESH)
 
+    loads_hi = [
+        load(band_hbm.at[middle], tiles.at[middle], 4),
+        load(panels_hbm.at[0, middle], rows.at[middle, :, first], 5),
+        load(panels_hbm.at[1, middle], rows.at[middle, :, second], 6),
+    ]
     loads_lo = [
-        load(panels_hbm.at[0, lower], rows.at[lower, :, first], 3),
-        load(panels_hbm.at[1, lower], rows.at[lower, :, second], 4),
-        load(band_hbm.at[lower], tiles.at[lower], 5),
-        load(seed_hbm.at[0], seeds.at[:, :, first], 6),
-        load(seed_hbm.at[1], seeds.at[:, :, second], 7),
+        load(panels_hbm.at[0, lower], rows.at[lower, :, first], 7),
+        load(panels_hbm.at[1, lower], rows.at[lower, :, second], 8),
+        load(band_hbm.at[lower], tiles.at[lower], 9),
+        load(seed_hbm.at[0], seeds.at[:, :, first], 10),
+        load(seed_hbm.at[1], seeds.at[:, :, second], 11),
     ]
     loads_last = [
-        load(inverse_hbm, diag_inverse, 9),
-        load(cross_hbm, cross_block, 10),
-        load(cross_seed_hbm, cross_seed, 11),
-        load(diag_seed_hbm, diag_seed, 12),
+        load(inverse_hbm, diag_inverse, 12),
+        load(cross_hbm, cross_block, 13),
+        load(cross_seed_hbm, cross_seed, 14),
+        load(diag_seed_hbm, diag_seed, 15),
     ]
 
     def tile(c, d):
@@ -187,16 +192,18 @@
                 )
             )
 
+    for copy in loads_edge:
+        copy.wait()
+    for r in (11, 10):
+        resid[r] = (-lower_terms(r, list(range(4, r - 8, -1)))).astype(BF16)
+
     pl.semaphore_wait(barrier, n_a + n_b)
     halos[0].start()
     halos[1].start()
-
+    parts[0].start()
+    parts[1].start()
     for copy in loads_hi:
         copy.wait()
-    for r in (11, 10):
-        resid[r] = (-lower_terms(r, list(range(4, r - 8, -1)))).astype(BF16)
-    parts[0].start()
-    parts[1].start()
     for r in (9, 8):
         resid[r] = (-lower_terms(r, list(range(4, r - 8, -1)))).astype(BF16)
 
@@ -284,6 +291,11 @@
 
     for p in range(2):
         begin = p * TILE
+        if p == 1:
+            lhs = [negm[i] for i in edge] + [rows[i, :, :TILE] for i in beyond]
+            rhs = [rows[i, :, begin : begin + TILE] for i in edge]
+            rhs += [resid[i, :, begin : begin + TILE] for i in beyond]
+            total[:, begin : begin + TILE] += dot_t(jnp.concatenate(lhs, axis=0), jnp.concatenate(rhs, axis=0))
         parts[p].wait_recv()
         for i in edge:
             arrived = left_in[i, :, begin : begin + TILE].astype(F32)
@@ -293,10 +305,13 @@
             if p == 0:
                 negm[i] = (negm[i].astype(F32) + arrived).astype(BF16)
         halos[p].wait_recv()
-        lhs = [rows[i, :, :TILE] for i in edge + beyond] + [negm[i] for i in edge]
-        lhs += [resid[i, :, :TILE] for i in beyond]
-        rhs = [resid[i, :, begin : begin + TILE] for i in edge + beyond]
-        rhs += [rows[i, :, begin : begin + TILE] for i in edge + beyond]
+        lhs = [rows[i, :, :TILE] for i in edge] + [resid[i, :, :TILE] for i in beyond]
+        rhs = [resid[i, :, begin : begin + TILE] for i in edge]
+        rhs += [rows[i, :, begin : begin + TILE] for i in beyond]
+        if p == 0:
+            lhs += [negm[i] for i in edge] + [rows[i, :, :TILE] for i in beyond]
+            rhs += [rows[i, :, begin : begin + TILE] for i in edge]
+            rhs += [resid[i, :, begin : begin + TILE] for i in beyond]
         value = total[:, begin : begin + TILE]
         value = value + dot_t(jnp.concatenate(lhs, axis=0), jnp.concatenate(rhs, axis=0))
         value = value.astype(BF16)
@@ -304,7 +319,7 @@
             staged[p, pl.ds(k * half, half)] = value[:, k * 128 : (k + 1) * 128].reshape(half, part_rows, 128)
         scatter(p)
 
-    for copy in halos[2:] + parts[2:]:
+    for copy in (halos[2], parts[2]):
         copy.start()
     for copy in loads_last:
         copy.wait()
@@ -341,6 +356,8 @@
 
     resid[pl.ds(2, 2)] = acc[pl.ds(2, 2)].astype(BF16)
     solve(2)
+    for copy in (halos[3], parts[3]):
+        copy.start()
     across(1)
 
     @pl.loop(4, 6)
@@ -447,7 +464,7 @@
             pltpu.VMEM((TILE, TILE), BF16),
             pltpu.VMEM((TILE, TILE), F32),
             pltpu.VMEM((TILE, TILE), F32),
-            dma((13,)),
+            dma((16,)),
             dma((2, 2)),
             dma((2, 2)),
             dma((2, 2)),

time: 41.4 us -> 40.2 us (0.971)
  Pallas kernels: 40.7 us -> 39.5 us
    pallas_call x1, Pallas kernels: 39.1 us -> 37.9 us  [body(): pl.pallas_call(functools.partial(kernel, n_col, plane_cols), out_shape=(p...]
where the time goes in v4:
time: 40.2 us; the launch traced here: 40.1 us
  Pallas kernels  39.5 us (98%)
  between operations  0.64 us (2%)
    pallas_call x1, Pallas kernels, body(): pl.pallas_call(functools.partial(kernel, n_col, plane_cols), out_shape=(p...  37.9 us
    pallas_call x1, Pallas kernels, body(): pl.pallas_call(functools.partial(finish, scale), out_shape=(jax.ShapeDtyp...  1.57 us

profile of v4, /device:TPU:1, one launch (start us, length us, event | category | flops | bytes accessed | tf_op | source)
XLA Modules:
  0.0 40.1 jit_solution(9877810648737186945)
XLA Ops:
  0.6 37.9 %shard_map.103 = (bf16[2,8,256,256]{3,2,1,0:T(8,128)(2,1)S(1)}, bf16[2,256,256]{2,1,0:T(8,128)(2,1)S(1)}, bf16[512,512]{1,0:T(8,128)(2,1)S(1)}, bf16[768,256]{1,...) custom-call(bf16[8,5,256,256]{3,2,1,0:T(8,128)(2,1)} %band_hbm.1, s32[8,5]{1,0:T(8,128)} %mask_hbm.1, ...), custom_call_target="tpu_custom_call" | custom-call | tf_op jit(solution)/shard_map/pallas_call | solution.py:434
  38.5 1.6 %shard_map.104 = (bf16[2,8,256,256]{3,2,1,0:T(8,128)(2,1)}, f32[256,256]{1,0:T(8,128)}, f32[256,256]{1,0:T(8,128)}) custom-call(bf16[2,8,256,256]{3,2,1,0:T(8,128)(2,1)S(1)} %get-tuple-element.9.out_v, bf16[2,256,256]{2,1,0:T(8,128)(2,1)S(1)} %get-tuple-element.10.sums, bf16[512,512]{1,0:T(8,128)(2,1)S(1)} %get-tuple-element.11.w_last, ...), custom_call_target="tpu_custom_call" | custom-call | tf_op jit(solution)/shard_map/pallas_call | solution.py:480
